TPU v7x, 512 devices: a whole 4x4x16 slice. The times are simulated.
512 devices in a mesh: seq: 64 (over z, y), head: 8 (over x, core).
Axes of the slice: x: 4, y: 4, z: 16, core: 2. Of those that a mesh axis runs over, the one named last changes fastest.
Arguments:
- queries: bfloat16 [81920, 2048], P('seq', 'head'), may hold values from -6 to 6
- keys: bfloat16 [81920, 2048], P('seq', 'head'), may hold values from -6 to 6
- values: bfloat16 [81920, 2048], P('seq', 'head'), may hold values from -6 to 6
- grad_out: bfloat16 [81920, 2048], P('seq', 'head'), may hold values from -6 to 6
Outputs:
- attended: bfloat16 [81920, 2048], P('seq', 'head')
- grad_queries: bfloat16 [81920, 2048], P('seq', 'head')
- grad_keys: bfloat16 [81920, 2048], P('seq', 'head')
- grad_values: bfloat16 [81920, 2048], P('seq', 'head')
All inputs are finite; a program needn't handle non-finite values.
Results may differ from a plain program's by a relative error of at most 0.0049.
Values sent between devices are 32-bit elements; how exact they have to be, the bound alone decides.
A program may use at most 64 MiB of HBM per device.

v0:
```python
import jax
import jax.numpy as jnp
from jax import lax
from jax.sharding import PartitionSpec as P

DH = 128
GROUP = 256


def entering(part, axis, combine, identity, reverse):
    count = lax.axis_size(axis)
    place = lax.axis_index(axis)
    ahead = count - 1 - place if reverse else place
    gathered = lax.all_gather(part, axis)
    state = jnp.zeros_like(part) + jnp.asarray(identity, part.dtype)

    def one(lap, state):
        source = count - 1 - lap if reverse else lap
        return combine(state, lax.dynamic_index_in_dim(gathered, source, 0, False))

    return lax.fori_loop(0, ahead, one, state)


def add_one(earlier, later):
    return earlier + later


def shards(queries, keys, values, grad_out):
    rows = queries.shape[0]
    width = queries.shape[1]
    count = width // DH
    total_tokens = rows * lax.axis_size("seq")
    scale = (DH * total_tokens) ** (-0.5)
    blocks = rows // GROUP
    qc = queries.reshape(blocks, GROUP, count, DH)
    kc = keys.reshape(blocks, GROUP, count, DH)
    vc = values.reshape(blocks, GROUP, count, DH)
    gc = grad_out.reshape(blocks, GROUP, count, DH)
    causal = lax.broadcasted_iota(jnp.int32, (GROUP, GROUP), 0) >= lax.broadcasted_iota(
        jnp.int32, (GROUP, GROUP), 1
    )
    states = jnp.einsum("cshd,cshe->chde", kc, vc, preferred_element_type=jnp.float32)
    grads_state = jnp.einsum("cthd,cthe->chde", qc, gc, preferred_element_type=jnp.float32)
    own_states = jnp.sum(states, axis=0)
    own_grads = jnp.sum(grads_state, axis=0)
    empty = jnp.zeros_like(own_states)
    earlier_sum = entering(own_states, "seq", add_one, empty, False)
    later_sum = entering(own_grads, "seq", add_one, empty, True)
    scores = jnp.einsum("cthd,cshd->chts", qc, kc, preferred_element_type=jnp.float32)
    probs = jnp.where(causal, scores * scale, 0.0).astype(jnp.bfloat16)
    dscores = jnp.einsum("cthe,cshe->chts", gc, vc, preferred_element_type=jnp.float32)
    dprobs = jnp.where(causal, dscores * scale, 0.0).astype(jnp.bfloat16)
    block_row = lax.broadcasted_iota(jnp.int32, (blocks, blocks), 0)
    block_col = lax.broadcasted_iota(jnp.int32, (blocks, blocks), 1)
    lower_ones = jnp.where(block_col < block_row, 1.0, 0.0).astype(jnp.float32)
    upper_ones = jnp.where(block_col > block_row, 1.0, 0.0).astype(jnp.float32)
    before = earlier_sum[None] + jnp.einsum(
        "bc,chde->bhde", lower_ones, states, precision=lax.Precision.HIGHEST
    )
    after = later_sum[None] + jnp.einsum(
        "bc,chde->bhde", upper_ones, grads_state, precision=lax.Precision.HIGHEST
    )
    before_low = before.astype(jnp.bfloat16)
    after_low = after.astype(jnp.bfloat16)
    attended = scale * jnp.einsum(
        "cthd,chde->cthe", qc, before_low, preferred_element_type=jnp.float32
    )
    attended = attended + jnp.einsum(
        "chts,cshe->cthe", probs, vc, preferred_element_type=jnp.float32
    )
    grad_q = scale * jnp.einsum(
        "cthe,chde->cthd", gc, before_low, preferred_element_type=jnp.float32
    )
    grad_q = grad_q + jnp.einsum("chts,cshd->cthd", dprobs, kc, preferred_element_type=jnp.float32)
    grad_k = scale * jnp.einsum(
        "cshe,chde->cshd", vc, after_low, preferred_element_type=jnp.float32
    )
    grad_k = grad_k + jnp.einsum("chts,cthd->cshd", dprobs, qc, preferred_element_type=jnp.float32)
    grad_v = scale * jnp.einsum(
        "cshd,chde->cshe", kc, after_low, preferred_element_type=jnp.float32
    )
    grad_v = grad_v + jnp.einsum("chts,cthe->cshe", probs, gc, preferred_element_type=jnp.float32)
    return (
        attended.reshape(rows, width).astype(jnp.bfloat16),
        grad_q.reshape(rows, width).astype(jnp.bfloat16),
        grad_k.reshape(rows, width).astype(jnp.bfloat16),
        grad_v.reshape(rows, width).astype(jnp.bfloat16),
    )


def solution(mesh):
    placed = (P("seq", "head"), P("seq", "head"), P("seq", "head"), P("seq", "head"))
    return jax.shard_map(
        shards,
        mesh=mesh,
        in_specs=placed,
        out_specs=(P("seq", "head"), P("seq", "head"), P("seq", "head"), P("seq", "head")),
        check_vma=False,
    )
```

profile of v0, /device:TPU:2, one launch (start us, length us, event | category | flops | bytes accessed | tf_op | source)
XLA Modules:
  0.0 419.0 jit_solution(1153693581152053755)
XLA Ops:
  7.2 1.9 reshape.30
  9.3 1.9 fusion.48
  11.6 1.0 fusion.49
  12.8 1.6 select_convert_fusion
  14.4 1.6 select_convert_fusion.1
  16.0 157.0 %all-gather.5.cloned.1.call-done = f32[128,128,128]{2,1,0:T(8,128)} async-done(((f32[2,128,128]{2,1,0:T(8,128)}), f32[128,128,128]{2,1,0:T(8,128)}) %all-gather.5.cloned.1.call-update) | async-done | bytes 8388624 | tf_op jit(solution)/shard_map/all_gather | solution.py:14
  173.0 2.4 fusion.12
  175.5 1.4 fusion.7
  176.9 1.5 fusion.6
  178.4 150.0 %all-gather.7.cloned.1.call-done = f32[128,128,128]{2,1,0:T(8,128)} async-done(((f32[2,128,128]{2,1,0:T(8,128)}), f32[128,128,128]{2,1,0:T(8,128)}) %all-gather.7.cloned.1.call-update) | async-done | bytes 8388624 | tf_op jit(solution)/shard_map/all_gather | solution.py:14
  328.4 60.5 %while.23 = (s32[]{:T(128)}, f32[2,128,128]{2,1,0:T(8,128)S(1)}, s32[]{:T(128)}, f32[64,2,128,128]{3,2,1,0:T(8,128)}, s32[]{:T(128)}, /*index=5*/s32[]{:T(128)}, s32[]{:T(128)}, s32[]{:T(128)}) while((s32[]{:T(128)}, f32[2,128,128]{2,1,0:T(8,128)S(1)}, s32[]{:T(128)}, f32[64,2,128,128]{3,2,1,0:T(8,128)}, s32[]{:T(128)}, /*index=5*/s32[]{:T(128)}, ...), condition=%wide.region_5.6_spmd, body=%wide.region_4.5_spmd.sunk | while | flops 32774 | bytes 393359 | solution.py:21
  388.8 2.2 fusion.13
  391.0 1.3 copy.94
  392.3 1.5 fusion.5
  393.8 1.4 fusion.4
  395.8 1.8 copy.77
  397.6 2.1 fusion.9
  399.7 1.8 copy.93
  401.5 2.7 fusion.10
  404.2 2.5 copy.84
  406.8 1.7 fusion.8
  408.5 1.1 copy.99
  409.6 1.3 copy_bitcast_fusion.2
  410.9 1.3 copy_bitcast_fusion
  (93 shorter events, 60.3 us)
Async XLA Ops:
  7.2 2.0 copy-start.6
  7.2 165.8 %all-gather.5.cloned.1.call-start = ((), (), s32[]{:S(2)}) async-start(), calls=%async_computation | async-start | bytes 8519680 | tf_op jit(solution)/shard_map/all_gather | solution.py:14
  9.3 2.0 copy-start.7
  9.3 2.1 copy-start.8
  11.3 317.1 %all-gather.7.cloned.1.call-start = ((), (), s32[]{:S(2)}) async-start(), calls=%async_computation.1 | async-start | bytes 8519680 | tf_op jit(solution)/shard_map/all_gather | solution.py:14
  392.3 2.9 copy-start.3
  393.8 1.4 copy-start.1
  399.7 1.8 copy-start
  404.2 2.6 copy-start.2
  408.5 1.1 copy-start.4
  409.6 1.3 copy-start.5
Sparse Core Ops, SparseCore 0:
  11.5 161.4 all-gather.4
  176.5 151.7 all-gather.6
where the time goes:
time: 421 us; the launch traced here: 419 us
  waiting for transfers between devices  307 us (73%)
  other arithmetic  59 us (14%)
  matrix products  23.7 us (6%)
  between operations  14.2 us (3%)
  local copies, waits for them, and re-layouts  13.5 us (3%)
    all_gather x2, waiting for transfers between devices, entering(): gathered = lax.all_gather(part, axis)  307 us
    add x63, other arithmetic, add_one(): return earlier + later  59 us
  transfers between devices with their start and end apart: 2, of which 2 were waited for; matrix products, arithmetic and copies ran while one was open for 2% of the time, Pallas kernels for 0%

commit v1 on v0

v1 whole, which is shorter than its diff:
```python
import functools

import jax
import jax.numpy as jnp
from jax import lax
from jax.experimental import pallas as pl
from jax.experimental.pallas import tpu as pltpu
from jax.sharding import PartitionSpec as P

DH = 128
GROUP = 256
MEMBERS = 8
MESH = pl.DeviceIdType.MESH


def dot(a, b, a_dim, b_dim):
    return lax.dot_general(a, b, (((a_dim,), (b_dim,)), ((), ())), preferred_element_type=jnp.float32)


def carry_kernel(
    scale, groups, q_hbm, k_hbm, v_hbm, g_hbm,
    q, k, v, g, part, inner, carry,
    load_sem, own, got, totals, far, back, send_sem, recv_sem,
):
    rows, width = q.shape
    blocks, heads = rows // GROUP, width // DH
    piece = heads * DH // MEMBERS
    head = lax.axis_index("head")
    me = lax.axis_index("seq")
    group, member = me // MEMBERS, lax.rem(me, MEMBERS)
    mates = [lax.rem(member + i, MEMBERS) for i in range(1, MEMBERS)]
    others = [lax.rem(group + i, groups) for i in range(1, groups)]

    def at(a_group, a_member):
        return (a_group * MEMBERS + a_member, head)

    barrier = pltpu.get_barrier_semaphore()
    for j in mates:
        pl.semaphore_signal(barrier, inc=1, device_id=at(group, j), device_id_type=MESH)
    for j in others:
        pl.semaphore_signal(barrier, inc=1, device_id=at(j, member), device_id_type=MESH)

    loads = [
        pltpu.make_async_copy(src, dst, load_sem.at[i])
        for i, (src, dst) in enumerate(((k_hbm, k), (v_hbm, v), (q_hbm, q), (g_hbm, g)))
    ]
    for load in loads:
        load.start()

    def head_of(ref, block, h):
        return ref[pl.ds(pl.multiple_of(block * GROUP, GROUP), GROUP), h * DH : (h + 1) * DH]

    def states(left, right, way, order):
        sums = [jnp.zeros((DH, DH), jnp.float32) for _ in range(heads)]
        for block in order:
            for h in range(heads):
                inner[way, block, h * DH : (h + 1) * DH, :] = sums[h]
                sums[h] = sums[h] + dot(head_of(left, block, h), head_of(right, block, h), 0, 0)
        for j in range(MEMBERS):
            h, row = divmod(j * piece, DH)
            own[j, way] = sums[h][row : row + piece]

    loads[0].wait()
    loads[1].wait()
    states(k, v, 0, range(blocks))
    loads[2].wait()
    loads[3].wait()
    states(q, g, 1, reversed(range(blocks)))
    pl.semaphore_wait(barrier, MEMBERS + groups - 2)

    def send(src, dst, step, target):
        return pltpu.make_async_remote_copy(
            src_ref=src, dst_ref=dst, send_sem=send_sem.at[step], recv_sem=recv_sem.at[step],
            device_id=target, device_id_type=MESH,
        )

    def arrive(buffer, count, step):
        ref = buffer.at[pl.ds(0, count)]
        pltpu.make_async_copy(ref, ref, recv_sem.at[step]).wait()

    def sent(buffer, count, step):
        ref = buffer.at[pl.ds(0, count)]
        pltpu.make_async_copy(ref, ref, send_sem.at[step]).wait()

    causal = lax.broadcasted_iota(jnp.int32, (GROUP, GROUP), 0) >= lax.broadcasted_iota(
        jnp.int32, (GROUP, GROUP), 1
    )

    def within(block, carried):
        here = pl.ds(pl.multiple_of(block * GROUP, GROUP), GROUP)
        for h in range(heads):
            cols = slice(h * DH, (h + 1) * DH)
            qb, kb, vb, gb = (head_of(ref, block, h) for ref in (q, k, v, g))
            probs = jnp.where(causal, dot(qb, kb, 1, 1) * scale, 0.0).astype(jnp.bfloat16)
            part[0, here, cols] = dot(probs, vb, 1, 0)
            part[3, here, cols] = dot(probs, gb, 0, 0)
            dprobs = jnp.where(causal, dot(gb, vb, 1, 1) * scale, 0.0).astype(jnp.bfloat16)
            part[1, here, cols] = dot(dprobs, kb, 1, 0)
            part[2, here, cols] = dot(dprobs, qb, 0, 0)
        return carried

    for j in mates:
        send(own.at[j], got.at[member], 0, at(group, j)).start()
    got[member] = own[member]
    lax.fori_loop(0, 2, within, 0)
    arrive(got, MEMBERS - 1, 0)
    total = got[0]
    for j in range(1, MEMBERS):
        total = total + got[j]
    totals[...] = total
    for j in others:
        way = jnp.where(j > group, 0, 1)
        send(totals.at[way], far.at[group], 1, at(j, member)).start()
    far[group] = jnp.zeros(far.shape[1:], jnp.float32)
    lax.fori_loop(2, 4, within, 0)
    arrive(far, groups - 1, 1)
    before = jnp.zeros(far.shape[1:], jnp.float32)
    after = jnp.zeros(far.shape[1:], jnp.float32)
    for j in range(groups):
        before = before + jnp.where(j < group, far[j], 0.0)
        after = after + jnp.where(j > group, far[j], 0.0)
    for j in range(MEMBERS):
        back[j, 0] = before
        before = before + got[j, 0]
    for j in reversed(range(MEMBERS)):
        back[j, 1] = after
        after = after + got[j, 1]
    for j in mates:
        send(back.at[j], carry.at[member], 2, at(group, j)).start()
    carry[member] = back[member]
    lax.fori_loop(4, blocks, within, 0)
    sent(own, MEMBERS - 1, 0)
    sent(far, groups - 1, 1)
    sent(back, MEMBERS - 1, 2)
    arrive(carry, MEMBERS - 1, 2)


def final_kernel(scale, q, k, v, g, part, inner, carry, *rest):
    outs, (weight, ready, sem) = rest[:4], rest[4:]
    rows, width = q.shape
    blocks, heads = rows // GROUP, width // DH
    zeros = jnp.zeros((DH, DH), jnp.bfloat16)
    stores = []
    for block in range(blocks):
        here = pl.ds(block * GROUP, GROUP)
        for way in range(2):
            entering = carry[:, way].reshape(heads * DH, DH) + inner[way, block]
            low = entering.astype(jnp.bfloat16)
            for h in range(heads):
                for other in range(heads):
                    weight[block, way, h * DH : (h + 1) * DH, other * DH : (other + 1) * DH] = (
                        low[h * DH : (h + 1) * DH] if h == other else zeros
                    )
        for i, (ref, way, dim) in enumerate(((q, 0, 0), (g, 0, 1), (v, 1, 1), (k, 1, 0))):
            value = scale * dot(ref[here], weight[block, way], 1, dim) + part[i, here]
            ready[i, here] = value.astype(jnp.bfloat16)
            store = pltpu.make_async_copy(ready.at[i, here], outs[i].at[here], sem.at[i, block])
            store.start()
            stores.append(store)
    for store in stores:
        store.wait()


def shards(queries, keys, values, grad_out):
    rows, width = queries.shape
    blocks, heads = rows // GROUP, width // DH
    count = lax.axis_size("seq")
    groups = count // MEMBERS
    piece = heads * DH // MEMBERS
    scale = (DH * rows * count) ** (-0.5)
    any_space = pl.BlockSpec(memory_space=pl.ANY)
    vmem = pl.BlockSpec(memory_space=pltpu.VMEM)
    f32 = jnp.float32
    low = pltpu.VMEM((rows, width), jnp.bfloat16)
    operands = [pltpu.with_memory_space_constraint(x, pltpu.HBM) for x in (queries, keys, values, grad_out)]
    held = pl.pallas_call(
        functools.partial(carry_kernel, scale, groups),
        out_shape=(
            low, low, low, low,
            pltpu.VMEM((4, rows, width), f32),
            pltpu.VMEM((2, blocks, heads * DH, DH), f32),
            pltpu.VMEM((MEMBERS, 2, piece, DH), f32),
        ),
        in_specs=[any_space] * 4,
        out_specs=(vmem,) * 7,
        scratch_shapes=[
            pltpu.SemaphoreType.DMA((4,)),
            pltpu.VMEM((MEMBERS, 2, piece, DH), f32),
            pltpu.VMEM((MEMBERS, 2, piece, DH), f32),
            pltpu.VMEM((2, piece, DH), f32),
            pltpu.VMEM((groups, piece, DH), f32),
            pltpu.VMEM((MEMBERS, 2, piece, DH), f32),
            pltpu.SemaphoreType.DMA((3,)),
            pltpu.SemaphoreType.DMA((3,)),
        ],
        compiler_params=pltpu.CompilerParams(
            collective_id=0, has_side_effects=True, vmem_limit_bytes=32 * 1024 * 1024
        ),
        name="scan_and_blocks",
    )(*operands)
    held = [pltpu.with_memory_space_constraint(x, pltpu.VMEM) for x in held]
    out = jax.ShapeDtypeStruct((rows, width), jnp.bfloat16)
    return pl.pallas_call(
        functools.partial(final_kernel, scale),
        out_shape=(out,) * 4,
        in_specs=[vmem] * 7,
        out_specs=(any_space,) * 4,
        scratch_shapes=[
            pltpu.VMEM((blocks, 2, width, width), jnp.bfloat16),
            pltpu.VMEM((4, rows, width), jnp.bfloat16),
            pltpu.SemaphoreType.DMA((4, blocks)),
        ],
        compiler_params=pltpu.CompilerParams(vmem_limit_bytes=32 * 1024 * 1024),
        name="across_blocks",
    )(*held)


def solution(mesh):
    placed = (P("seq", "head"),) * 4
    return jax.shard_map(shards, mesh=mesh, in_specs=placed, out_specs=placed, check_vma=False)
```

time: 421 us -> 35.6 us (0.08)
  the two profiles are of different devices: /device:TPU:2 before, /device:TPU:4 now
where the time goes in v1:
time: 35.6 us; the launch traced here: 35.5 us
  Pallas kernels  34.8 us (98%)
  between operations  0.64 us (2%)
    pallas_call x1, Pallas kernels, shards(): pl.pallas_call(functools.partial(carry_kernel, scale, groups), out_shape=...  32.8 us
    pallas_call x1, Pallas kernels, shards(): pl.pallas_call(functools.partial(final_kernel, scale), out_shape=(out,) *...  2.08 us

profile of v1, /device:TPU:4, one launch (start us, length us, event | category | flops | bytes accessed | tf_op | source)
XLA Modules:
  0.0 35.5 jit_solution(18175876757375681405)
XLA Ops:
  0.6 32.8 %scan_and_blocks.1 = (bf16[1280,256]{1,0:T(8,128)(2,1)S(1)}, bf16[1280,256]{1,0:T(8,128)(2,1)S(1)}, bf16[1280,256]{1,0:T(8,128)(2,1)S(1)}, bf16[1280,256]{1,0:T(...) custom-call(bf16[1280,256]{1,0:T(8,128)(2,1)} %q_hbm.1, ...), custom_call_target="tpu_custom_call" | custom-call | tf_op jit(solution)/shard_map/scan_and_blocks/pallas_call | solution.py:176
  33.4 2.1 %across_blocks.1 = (bf16[1280,256]{1,0:T(8,128)(2,1)}, bf16[1280,256]{1,0:T(8,128)(2,1)}, bf16[1280,256]{1,0:T(8,128)(2,1)}, bf16[1280,256]{1,0:T(8,128)(2,1)}) custom-call(bf16[1280,256]{1,0:T(8,128)(2,1)S(1)} %get-tuple-element.11.q, bf16[1280,256]{1,0:T(8,128)(2,1)S(1)} %get-tuple-element.12.k, bf16[1280,256]{1,0:T(8,128)(2,1)S(1)} %get-tuple-element.13.v, ...), custom_call_target="tpu_custom_call" | custom-call | tf_op jit(solution)/shard_map/across_blocks/pallas_call | solution.py:203

commit v2 on v1

v2 whole, which is shorter than its diff:
```python
import functools

import jax
import jax.numpy as jnp
from jax import lax
from jax.experimental import pallas as pl
from jax.experimental.pallas import tpu as pltpu
from jax.sharding import PartitionSpec as P

DH = 128
GROUP = 256
MEMBERS = 8
BEFORE, AFTER = 0, 1
MESH = pl.DeviceIdType.MESH


def dot(a, b, a_dim, b_dim):
    return lax.dot_general(a, b, (((a_dim,), (b_dim,)), ((), ())), preferred_element_type=jnp.float32)


def across(scale, refs, dims, entering, inner, part, weight, ready, done=None):
    rows, width = refs[0].shape
    heads = width // DH
    zeros = jnp.zeros((DH, DH), jnp.bfloat16)
    state = entering[...].reshape(heads * DH, DH)
    for block in range(rows // GROUP):
        here = pl.ds(block * GROUP, GROUP)
        low = (state + inner[block]).astype(jnp.bfloat16)
        for h in range(heads):
            for other in range(heads):
                weight[block, h * DH : (h + 1) * DH, other * DH : (other + 1) * DH] = (
                    low[h * DH : (h + 1) * DH] if h == other else zeros
                )
        for i, (ref, dim) in enumerate(zip(refs, dims, strict=True)):
            value = scale * dot(ref[here], weight[block], 1, dim) + part[i, here]
            ready[i, here] = value.astype(jnp.bfloat16)
            if done is not None:
                done(i, block)


def carry_kernel(
    scale, groups, q_hbm, k_hbm, v_hbm, g_hbm,
    k, v, early, part, inner, carry,
    q, g, early_part, early_inner, early_carry, weight, own, got, totals, far, back,
    load_sem, send_sem, recv_sem, far_sem, higher_sem,
):
    rows, width = q.shape
    blocks, heads = rows // GROUP, width // DH
    piece = heads * DH // MEMBERS
    head = lax.axis_index("head")
    me = lax.axis_index("seq")
    group, member = me // MEMBERS, lax.rem(me, MEMBERS)
    mates = [lax.rem(member + i, MEMBERS) for i in (6, 2, 5, 1, 7, 3, 4)]
    inners, carries = (early_inner, inner), (early_carry, carry)

    def at(a_group, a_member):
        return (a_group * MEMBERS + a_member, head)

    def tell(sem, target):
        pl.semaphore_signal(sem, inc=1, device_id=target, device_id_type=MESH)

    loads = [
        pltpu.make_async_copy(src, dst, load_sem.at[i])
        for i, (src, dst) in enumerate(((q_hbm, q), (g_hbm, g), (k_hbm, k), (v_hbm, v)))
    ]
    loads[0].start()
    loads[1].start()
    far[...] = jnp.zeros_like(far)
    barrier = pltpu.get_barrier_semaphore()
    for j in mates:
        tell(barrier, at(group, j))
    for j in range(1, groups):

        @pl.when(j > group)
        def _():
            tell(barrier, at(j, member))

    def states(left, right, way, order):
        sums = [jnp.zeros((DH, DH), jnp.float32) for _ in range(heads)]
        for block in order:
            here = slice(block * GROUP, (block + 1) * GROUP)
            for h in range(heads):
                cols = slice(h * DH, (h + 1) * DH)
                inners[way][block, cols] = sums[h]
                sums[h] = sums[h] + dot(left[here, cols], right[here, cols], 0, 0)
        for j in range(MEMBERS):
            h, row = divmod(j * piece, DH)
            own[way, j] = sums[h][row : row + piece]

    def send(src, dst, send_at, recv_at, target):
        pltpu.make_async_remote_copy(
            src_ref=src, dst_ref=dst, send_sem=send_at, recv_sem=recv_at,
            device_id=target, device_id_type=MESH,
        ).start()

    def wait(ref, sem):
        pltpu.make_async_copy(ref, ref, sem).wait()

    def answer():
        for j in range(groups - 1):

            @pl.when(j < group)
            def _():
                tell(higher_sem, at(j, member))

    def scatter(way):
        for j in mates:
            send(own.at[way, j], got.at[way, member], send_sem.at[way, 0], recv_sem.at[way, 0], at(group, j))
        got[way, member] = own[way, member]

    def exchange(way):
        wait(got.at[way, pl.ds(0, MEMBERS - 1)], recv_sem.at[way, 0])
        total = got[way, 0]
        for j in range(1, MEMBERS):
            total = total + got[way, j]
        totals[way] = total
        if way == BEFORE:

            @pl.when(group < groups - 1)
            def _():
                pl.semaphore_wait(higher_sem, groups - 1 - group)

        for j in range(groups):

            @pl.when(j > group if way == BEFORE else j < group)
            def _():
                send(
                    totals.at[way], far.at[way, group], send_sem.at[0, 1], far_sem.at[way, group],
                    at(j, member),
                )

    def give_back(way):
        for j in range(groups):

            @pl.when(j < group if way == BEFORE else j > group)
            def _():
                wait(far.at[way, j], far_sem.at[way, j])

        total = jnp.zeros((piece, DH), jnp.float32)
        for j in range(groups):
            total = total + jnp.where(j < group if way == BEFORE else j > group, far[way, j], 0.0)
        for j in range(MEMBERS) if way == BEFORE else reversed(range(MEMBERS)):
            back[way, j] = total
            total = total + got[way, j]
        for j in mates:
            send(back.at[way, j], carries[way].at[member], send_sem.at[way, 2], recv_sem.at[way, 2], at(group, j))
        carries[way][member] = back[way, member]

    causal = lax.broadcasted_iota(jnp.int32, (GROUP, GROUP), 0) >= lax.broadcasted_iota(
        jnp.int32, (GROUP, GROUP), 1
    )

    def within(block, carried):
        here = pl.ds(pl.multiple_of(block * GROUP, GROUP), GROUP)
        for h in range(heads):
            cols = slice(h * DH, (h + 1) * DH)
            qb, kb, vb, gb = (ref[here, cols] for ref in (q, k, v, g))
            probs = jnp.where(causal, dot(qb, kb, 1, 1) * scale, 0.0).astype(jnp.bfloat16)
            early_part[0, here, cols] = dot(probs, vb, 1, 0)
            part[1, here, cols] = dot(probs, gb, 0, 0)
            dprobs = jnp.where(causal, dot(gb, vb, 1, 1) * scale, 0.0).astype(jnp.bfloat16)
            early_part[1, here, cols] = dot(dprobs, kb, 1, 0)
            part[0, here, cols] = dot(dprobs, qb, 0, 0)
        return carried

    loads[0].wait()
    loads[1].wait()
    loads[2].start()
    loads[3].start()
    states(q, g, AFTER, reversed(range(blocks)))
    pl.semaphore_wait(barrier, MEMBERS - 1 + group)
    scatter(AFTER)
    answer()
    loads[2].wait()
    loads[3].wait()
    states(k, v, BEFORE, range(blocks))
    scatter(BEFORE)
    exchange(AFTER)
    lax.fori_loop(0, blocks, within, 0)
    exchange(BEFORE)
    give_back(BEFORE)
    give_back(AFTER)
    wait(early_carry.at[pl.ds(0, MEMBERS - 1)], recv_sem.at[BEFORE, 2])
    across(scale, (q, g), (0, 1), early_carry, early_inner, early_part, weight, early)
    wait(far.at[0, pl.ds(0, groups - 1)], send_sem.at[0, 1])
    for way in (BEFORE, AFTER):
        wait(own.at[way, pl.ds(0, MEMBERS - 1)], send_sem.at[way, 0])
        wait(back.at[way, pl.ds(0, MEMBERS - 1)], send_sem.at[way, 2])
    wait(carry.at[pl.ds(0, MEMBERS - 1)], recv_sem.at[AFTER, 2])


def final_kernel(scale, k, v, early, part, inner, carry, *rest):
    outs, (weight, ready, early_sem, sem) = rest[:4], rest[4:]
    stores = [pltpu.make_async_copy(early.at[i], outs[i], early_sem.at[i]) for i in range(2)]
    for store in stores:
        store.start()

    def done(i, block):
        here = pl.ds(block * GROUP, GROUP)
        store = pltpu.make_async_copy(ready.at[i, here], outs[2 + i].at[here], sem.at[i, block])
        store.start()
        stores.append(store)

    across(scale, (v, k), (1, 0), carry, inner, part, weight, ready, done)
    for store in stores:
        store.wait()


def shards(queries, keys, values, grad_out):
    rows, width = queries.shape
    blocks, heads = rows // GROUP, width // DH
    count = lax.axis_size("seq")
    groups = count // MEMBERS
    piece = heads * DH // MEMBERS
    scale = (DH * rows * count) ** (-0.5)
    anywhere = pl.BlockSpec(memory_space=pl.ANY)
    vmem = pl.BlockSpec(memory_space=pltpu.VMEM)
    f32 = jnp.float32
    array = pltpu.VMEM((rows, width), jnp.bfloat16)
    pair = pltpu.VMEM((2, rows, width), jnp.bfloat16)
    parts = pltpu.VMEM((2, rows, width), f32)
    inner = pltpu.VMEM((blocks, heads * DH, DH), f32)
    carry = pltpu.VMEM((MEMBERS, piece, DH), f32)
    weight = pltpu.VMEM((blocks, width, width), jnp.bfloat16)
    pieces = pltpu.VMEM((2, MEMBERS, piece, DH), f32)
    dma = pltpu.SemaphoreType.DMA
    operands = [
        pltpu.with_memory_space_constraint(x, pltpu.HBM) for x in (queries, keys, values, grad_out)
    ]
    held = pl.pallas_call(
        functools.partial(carry_kernel, scale, groups),
        out_shape=(array, array, pair, parts, inner, carry),
        in_specs=[anywhere] * 4,
        out_specs=(vmem,) * 6,
        scratch_shapes=[
            array, array, parts, inner, carry, weight,
            pieces, pieces, pltpu.VMEM((2, piece, DH), f32), pltpu.VMEM((2, groups, piece, DH), f32), pieces,
            dma((4,)), dma((2, 3)), dma((2, 3)), dma((2, groups)),
            pltpu.SemaphoreType.REGULAR,
        ],
        compiler_params=pltpu.CompilerParams(
            collective_id=0, has_side_effects=True, vmem_limit_bytes=32 * 1024 * 1024
        ),
        name="scan_and_blocks",
    )(*operands)
    held = [pltpu.with_memory_space_constraint(x, pltpu.VMEM) for x in held]
    out = jax.ShapeDtypeStruct((rows, width), jnp.bfloat16)
    return pl.pallas_call(
        functools.partial(final_kernel, scale),
        out_shape=(out,) * 4,
        in_specs=[vmem] * 6,
        out_specs=(anywhere,) * 4,
        scratch_shapes=[weight, pair, dma((2,)), dma((2, blocks))],
        compiler_params=pltpu.CompilerParams(vmem_limit_bytes=32 * 1024 * 1024),
        name="across_blocks",
    )(*held)


def solution(mesh):
    placed = (P("seq", "head"),) * 4
    return jax.shard_map(shards, mesh=mesh, in_specs=placed, out_specs=placed, check_vma=False)
```

time: 35.6 us -> 32.2 us (0.904)
  the two profiles are of different devices: /device:TPU:4 before, /device:TPU:2 now
where the time goes in v2:
time: 32.2 us; the launch traced here: 32.1 us
  Pallas kernels  31.4 us (98%)
  between operations  0.64 us (2%)
    pallas_call x1, Pallas kernels, shards(): pl.pallas_call(functools.partial(carry_kernel, scale, groups), out_shape=...  29.5 us
    pallas_call x1, Pallas kernels, shards(): pl.pallas_call(functools.partial(final_kernel, scale), out_shape=(out,) *...  1.91 us

profile of v2, /device:TPU:2, one launch (start us, length us, event | category | flops | bytes accessed | tf_op | source)
XLA Modules:
  0.0 32.1 jit_solution(8913149713440375576)
XLA Ops:
  0.6 29.5 %scan_and_blocks.1 = (bf16[1280,256]{1,0:T(8,128)(2,1)S(1)}, bf16[1280,256]{1,0:T(8,128)(2,1)S(1)}, bf16[2,1280,256]{2,1,0:T(8,128)(2,1)S(1)}, f32[2,1280,256]{2...) custom-call(bf16[1280,256]{1,0:T(8,128)(2,1)} %q_hbm.1, bf16[1280,256]{1,0:T(8,128)(2,1)} %k_hbm.1, ...), custom_call_target="tpu_custom_call" | custom-call | tf_op jit(solution)/shard_map/scan_and_blocks/pallas_call | solution.py:230
  30.2 1.9 %across_blocks.1 = (bf16[1280,256]{1,0:T(8,128)(2,1)}, bf16[1280,256]{1,0:T(8,128)(2,1)}, bf16[1280,256]{1,0:T(8,128)(2,1)}, bf16[1280,256]{1,0:T(8,128)(2,1)}) custom-call(bf16[1280,256]{1,0:T(8,128)(2,1)S(1)} %get-tuple-element.10.k, bf16[1280,256]{1,0:T(8,128)(2,1)S(1)} %get-tuple-element.11.v, bf16[2,1280,256]{2,1,0:T(8,128)(2,1)S(1)} %get-tuple-element.12.early, ...), custom_call_target="tpu_custom_call" | custom-call | tf_op jit(solution)/shard_map/across_blocks/pallas_call | solution.py:248

commit v3 on v2

v3 whole, which is shorter than its diff:
```python
import functools

import jax
import jax.numpy as jnp
from jax import lax
from jax.experimental import pallas as pl
from jax.experimental.pallas import tpu as pltpu
from jax.sharding import PartitionSpec as P

DH = 128
GROUP = 256
MEMBERS = 8
BEFORE, AFTER = 0, 1
MESH = pl.DeviceIdType.MESH


def dot(a, b, a_dim, b_dim):
    return lax.dot_general(a, b, (((a_dim,), (b_dim,)), ((), ())), preferred_element_type=jnp.float32)


def across(scale, refs, dims, entering, inner, part, ready, done=None):
    rows, width = refs[0].shape
    state = entering[...].reshape(width, DH)
    for block in range(rows // GROUP):
        here = pl.ds(block * GROUP, GROUP)
        low = (state + inner[block]).astype(jnp.bfloat16)
        for i, (ref, dim) in enumerate(zip(refs, dims, strict=True)):
            for h in range(width // DH):
                cols = slice(h * DH, (h + 1) * DH)
                value = scale * dot(ref[here, cols], low[cols], 1, dim) + part[i, here, cols]
                ready[i, here, cols] = value.astype(jnp.bfloat16)
            if done is not None:
                done(i, block)


def carry_kernel(
    scale, groups, q_hbm, k_hbm, v_hbm, g_hbm,
    k, v, early, part, inner, carry,
    q, g, early_part, early_inner, early_carry, sums, own, got, totals, half_sum, far, back,
    load_sem, send_sem, recv_sem, far_send_sem, far_sem, higher_sem,
):
    rows, width = q.shape
    blocks, heads = rows // GROUP, width // DH
    piece = heads * DH // MEMBERS
    head = lax.axis_index("head")
    me = lax.axis_index("seq")
    group, member = me // MEMBERS, lax.rem(me, MEMBERS)
    mates = [lax.rem(member + i, MEMBERS) for i in (6, 2, 5, 1, 7, 3, 4)]
    half, near = groups // 2, groups // 2 - 1
    turn = MEMBERS // 2

    def turned(a_group, index):
        return lax.rem(index + jnp.where(a_group == half, turn, 0), MEMBERS)

    mine = turned(group, member)
    inners, carries = (early_inner, inner), (early_carry, carry)

    def at(a_group, a_member):
        return (a_group * MEMBERS + a_member, head)

    def tell(sem, target):
        pl.semaphore_signal(sem, inc=1, device_id=target, device_id_type=MESH)

    barrier = pltpu.get_barrier_semaphore()
    for j in mates:
        tell(barrier, at(group, j))
    for j in range(groups):

        @pl.when((j > group) & ((group < near) | (group >= half) | (j <= half)))
        def _():
            tell(barrier, at(j, turned(j, mine)))

    loads = [
        pltpu.make_async_copy(src, dst, load_sem.at[i])
        for i, (src, dst) in enumerate(((q_hbm, q), (g_hbm, g), (k_hbm, k), (v_hbm, v)))
    ]
    loads[0].start()
    loads[1].start()
    sums[...] = jnp.zeros_like(sums)

    def states(left, right, way, order):
        sums = [jnp.zeros((DH, DH), jnp.float32) for _ in range(heads)]
        for block in order:
            here = slice(block * GROUP, (block + 1) * GROUP)
            for h in range(heads):
                cols = slice(h * DH, (h + 1) * DH)
                inners[way][block, cols] = sums[h]
                sums[h] = sums[h] + dot(left[here, cols], right[here, cols], 0, 0)
        for j in range(MEMBERS):
            h, row = divmod(j * piece, DH)
            own[way, j] = sums[h][row : row + piece]

    def send(src, dst, send_at, recv_at, target):
        pltpu.make_async_remote_copy(
            src_ref=src, dst_ref=dst, send_sem=send_at, recv_sem=recv_at,
            device_id=target, device_id_type=MESH,
        ).start()

    def wait(ref, sem):
        pltpu.make_async_copy(ref, ref, sem).wait()

    def answer():
        for j in range(groups):

            @pl.when((j < group) & ((group < half) | (j >= half)))
            def _():
                tell(higher_sem, at(j, turned(j, mine)))

    def scatter(way):
        for j in mates:
            send(
                own.at[way, turned(group, j)], got.at[way, member], send_sem.at[way, 0], recv_sem.at[way, 0], at(group, j)
            )
        got[way, member] = own[way, mine]

    def collect(way):
        wait(got.at[way, pl.ds(0, MEMBERS - 1)], recv_sem.at[way, 0])
        total = got[way, 0]
        for j in range(1, MEMBERS):
            total = total + got[way, j]
        totals[way] = total

    def send_far(src, way, j):
        send(src, far.at[way, group], far_send_sem.at[way, j], far_sem.at[way, group], at(j, turned(j, mine)))

    def direct(way, j):
        if way == BEFORE:
            return (j > group) & ((group >= half) | (j < half))
        return (j < group) & ((group < half) | (j < near) | (j >= half))

    def summed(way, j):
        if way == BEFORE:
            return (group == half - 1) & (j >= half)
        return (group == half) & (near <= j < half)

    def exchange(way):
        for j in range(groups):

            @pl.when(direct(way, j))
            def _():
                send_far(totals.at[way], way, j)

    def gather(way):
        for j in range(groups) if way == BEFORE else reversed(range(groups)):
            here = (j < group) & ((group < half) | (j >= half - 1))
            if way == AFTER:
                here = (j > group) & ((group < near) | (group >= half) | (j <= half))

            @pl.when(here)
            def _():
                wait(far.at[way, j], far_sem.at[way, j])
                sums[way] += far[way, j]

    def exchange_sum(way):
        @pl.when(group == (half - 1 if way == BEFORE else half))
        def _():
            half_sum[way] = sums[way] + totals[way]
            for j in range(groups):

                @pl.when(summed(way, j))
                def _():
                    send_far(half_sum.at[way], way, j)

    def give_back(way):
        total = sums[way]
        for j in range(MEMBERS) if way == BEFORE else reversed(range(MEMBERS)):
            back[way, j] = total
            total = total + got[way, j]
        for j in mates:
            send(back.at[way, j], carries[way].at[mine], send_sem.at[way, 1], recv_sem.at[way, 1], at(group, j))
        carries[way][mine] = back[way, member]

    causal = lax.broadcasted_iota(jnp.int32, (GROUP, GROUP), 0) >= lax.broadcasted_iota(
        jnp.int32, (GROUP, GROUP), 1
    )

    def within(block, carried):
        here = pl.ds(pl.multiple_of(block * GROUP, GROUP), GROUP)
        for h in range(heads):
            cols = slice(h * DH, (h + 1) * DH)
            qb, kb, vb, gb = (ref[here, cols] for ref in (q, k, v, g))
            probs = jnp.where(causal, dot(qb, kb, 1, 1) * scale, 0.0).astype(jnp.bfloat16)
            early_part[0, here, cols] = dot(probs, vb, 1, 0)
            part[1, here, cols] = dot(probs, gb, 0, 0)
            dprobs = jnp.where(causal, dot(gb, vb, 1, 1) * scale, 0.0).astype(jnp.bfloat16)
            early_part[1, here, cols] = dot(dprobs, kb, 1, 0)
            part[0, here, cols] = dot(dprobs, qb, 0, 0)
        return carried

    loads[0].wait()
    loads[1].wait()
    loads[2].start()
    loads[3].start()
    states(q, g, AFTER, reversed(range(blocks)))
    pl.semaphore_wait(barrier, MEMBERS - 1 + jnp.where(group <= half, group, near + group - half))
    scatter(AFTER)
    answer()
    loads[2].wait()
    loads[3].wait()
    states(k, v, BEFORE, range(blocks))
    scatter(BEFORE)
    collect(AFTER)
    exchange(AFTER)

    @pl.when(group == half)
    def _():
        pl.semaphore_wait(higher_sem, groups - 1 - half)
        tell(higher_sem, at(half - 1, turned(half - 1, mine)))

    lax.fori_loop(0, 3, within, 0)
    collect(BEFORE)
    higher = jnp.where(group < half - 1, half - 1 - group, jnp.where(group == half - 1, 1, groups - 1 - group))

    @pl.when((group != half) & (group < groups - 1))
    def _():
        pl.semaphore_wait(higher_sem, higher)

    exchange(BEFORE)

    @pl.when(group < half)
    def _():
        gather(BEFORE)
        exchange_sum(BEFORE)
        give_back(BEFORE)

    lax.fori_loop(3, blocks, within, 0)

    @pl.when(group >= half)
    def _():
        gather(AFTER)
        exchange_sum(AFTER)
        give_back(AFTER)

    @pl.when(group >= half)
    def _():
        gather(BEFORE)
        give_back(BEFORE)

    @pl.when(group < half)
    def _():
        gather(AFTER)
        give_back(AFTER)

    wait(early_carry.at[pl.ds(0, MEMBERS - 1)], recv_sem.at[BEFORE, 1])
    across(scale, (q, g), (0, 1), early_carry, early_inner, early_part, early)
    for way in (BEFORE, AFTER):
        for j in range(groups):

            @pl.when(direct(way, j) | summed(way, j))
            def _():
                wait(totals.at[way], far_send_sem.at[way, j])

        wait(own.at[way, pl.ds(0, MEMBERS - 1)], send_sem.at[way, 0])
        wait(back.at[way, pl.ds(0, MEMBERS - 1)], send_sem.at[way, 1])
    wait(carry.at[pl.ds(0, MEMBERS - 1)], recv_sem.at[AFTER, 1])


def final_kernel(scale, k, v, early, part, inner, carry, *rest):
    outs, (ready, early_sem, sem) = rest[:4], rest[4:]
    stores = [pltpu.make_async_copy(early.at[i], outs[i], early_sem.at[i]) for i in range(2)]
    for store in stores:
        store.start()

    def done(i, block):
        here = pl.ds(block * GROUP, GROUP)
        store = pltpu.make_async_copy(ready.at[i, here], outs[2 + i].at[here], sem.at[i, block])
        store.start()
        stores.append(store)

    across(scale, (v, k), (1, 0), carry, inner, part, ready, done)
    for store in stores:
        store.wait()


def shards(queries, keys, values, grad_out):
    rows, width = queries.shape
    blocks, heads = rows // GROUP, width // DH
    count = lax.axis_size("seq")
    groups = count // MEMBERS
    piece = heads * DH // MEMBERS
    scale = (DH * rows * count) ** (-0.5)
    anywhere = pl.BlockSpec(memory_space=pl.ANY)
    vmem = pl.BlockSpec(memory_space=pltpu.VMEM)
    f32 = jnp.float32
    array = pltpu.VMEM((rows, width), jnp.bfloat16)
    pair = pltpu.VMEM((2, rows, width), jnp.bfloat16)
    parts = pltpu.VMEM((2, rows, width), f32)
    inner = pltpu.VMEM((blocks, heads * DH, DH), f32)
    carry = pltpu.VMEM((MEMBERS, piece, DH), f32)
    pieces = pltpu.VMEM((2, MEMBERS, piece, DH), f32)
    dma = pltpu.SemaphoreType.DMA
    operands = [
        pltpu.with_memory_space_constraint(x, pltpu.HBM) for x in (queries, keys, values, grad_out)
    ]
    held = pl.pallas_call(
        functools.partial(carry_kernel, scale, groups),
        out_shape=(array, array, pair, parts, inner, carry),
        in_specs=[anywhere] * 4,
        out_specs=(vmem,) * 6,
        scratch_shapes=[
            array, array, parts, inner, carry, pltpu.VMEM((2, piece, DH), f32),
            pieces, pieces, pltpu.VMEM((2, piece, DH), f32), pltpu.VMEM((2, piece, DH), f32),
            pltpu.VMEM((2, groups, piece, DH), f32), pieces,
            dma((4,)), dma((2, 2)), dma((2, 2)), dma((2, groups)), dma((2, groups)),
            pltpu.SemaphoreType.REGULAR,
        ],
        compiler_params=pltpu.CompilerParams(
            collective_id=0, has_side_effects=True, vmem_limit_bytes=32 * 1024 * 1024
        ),
        name="scan_and_blocks",
    )(*operands)
    held = [pltpu.with_memory_space_constraint(x, pltpu.VMEM) for x in held]
    out = jax.ShapeDtypeStruct((rows, width), jnp.bfloat16)
    return pl.pallas_call(
        functools.partial(final_kernel, scale),
        out_shape=(out,) * 4,
        in_specs=[vmem] * 6,
        out_specs=(anywhere,) * 4,
        scratch_shapes=[pair, dma((2,)), dma((2, blocks))],
        compiler_params=pltpu.CompilerParams(vmem_limit_bytes=32 * 1024 * 1024),
        name="across_blocks",
    )(*held)


def solution(mesh):
    placed = (P("seq", "head"),) * 4
    return jax.shard_map(shards, mesh=mesh, in_specs=placed, out_specs=placed, check_vma=False)
```

time: 32.2 us -> 31.5 us (0.978)
  the two profiles are of different devices: /device:TPU:2 before, /device:TPU:66 now
where the time goes in v3:
time: 31.5 us; the launch traced here: 31.3 us
  Pallas kernels  30.7 us (97%)
  between operations  0.64 us (2%)
    pallas_call x1, Pallas kernels, shards(): pl.pallas_call(functools.partial(carry_kernel, scale, groups), out_shape=...  28.9 us
    pallas_call x1, Pallas kernels, shards(): pl.pallas_call(functools.partial(final_kernel, scale), out_shape=(out,) *...  1.8 us

profile of v3, /device:TPU:66, one launch (start us, length us, event | category | flops | bytes accessed | tf_op | source)
XLA Modules:
  0.0 31.3 jit_solution(2192509306923227945)
XLA Ops:
  0.6 28.9 %scan_and_blocks.1 = (bf16[1280,256]{1,0:T(8,128)(2,1)S(1)}, bf16[1280,256]{1,0:T(8,128)(2,1)S(1)}, bf16[2,1280,256]{2,1,0:T(8,128)(2,1)S(1)}, f32[2,1280,256]{2...) custom-call(bf16[1280,256]{1,0:T(8,128)(2,1)} %q_hbm.1, bf16[1280,256]{1,0:T(8,128)(2,1)} %k_hbm.1, ...), custom_call_target="tpu_custom_call" | custom-call | tf_op jit(solution)/shard_map/scan_and_blocks/pallas_call | solution.py:295
  29.5 1.8 %across_blocks.1 = (bf16[1280,256]{1,0:T(8,128)(2,1)}, bf16[1280,256]{1,0:T(8,128)(2,1)}, bf16[1280,256]{1,0:T(8,128)(2,1)}, bf16[1280,256]{1,0:T(8,128)(2,1)}) custom-call(bf16[1280,256]{1,0:T(8,128)(2,1)S(1)} %get-tuple-element.10.k, bf16[1280,256]{1,0:T(8,128)(2,1)S(1)} %get-tuple-element.11.v, bf16[2,1280,256]{2,1,0:T(8,128)(2,1)S(1)} %get-tuple-element.12.early, ...), custom_call_target="tpu_custom_call" | custom-call | tf_op jit(solution)/shard_map/across_blocks/pallas_call | solution.py:314

commit v4 on v3

--- a/solution.py
+++ b/solution.py
@@ -207,7 +207,7 @@
         pl.semaphore_wait(higher_sem, groups - 1 - half)
         tell(higher_sem, at(half - 1, turned(half - 1, mine)))
 
-    lax.fori_loop(0, 3, within, 0)
+    lax.fori_loop(0, 2, within, 0)
     collect(BEFORE)
     higher = jnp.where(group < half - 1, half - 1 - group, jnp.where(group == half - 1, 1, groups - 1 - group))
 
@@ -223,7 +223,7 @@
         exchange_sum(BEFORE)
         give_back(BEFORE)
 
-    lax.fori_loop(3, blocks, within, 0)
+    lax.fori_loop(2, blocks, within, 0)
 
     @pl.when(group >= half)
     def _():

time: 31.5 us -> 31.3 us (level)
  the two profiles are of different devices: /device:TPU:66 before, /device:TPU:68 now
where the time goes in v4:
time: 31.3 us; the launch traced here: 31.1 us
  Pallas kernels  30.5 us (97%)
  between operations  0.64 us (2%)
    pallas_call x1, Pallas kernels, shards(): pl.pallas_call(functools.partial(carry_kernel, scale, groups), out_shape=...  28.7 us
    pallas_call x1, Pallas kernels, shards(): pl.pallas_call(functools.partial(final_kernel, scale), out_shape=(out,) *...  1.8 us

profile of v4, /device:TPU:68, one launch (start us, length us, event | category | flops | bytes accessed | tf_op | source)
XLA Modules:
  0.0 31.1 jit_solution(1421450262528070416)
XLA Ops:
  0.6 28.7 %scan_and_blocks.1 = (bf16[1280,256]{1,0:T(8,128)(2,1)S(1)}, bf16[1280,256]{1,0:T(8,128)(2,1)S(1)}, bf16[2,1280,256]{2,1,0:T(8,128)(2,1)S(1)}, f32[2,1280,256]{2...) custom-call(bf16[1280,256]{1,0:T(8,128)(2,1)} %q_hbm.1, bf16[1280,256]{1,0:T(8,128)(2,1)} %k_hbm.1, ...), custom_call_target="tpu_custom_call" | custom-call | tf_op jit(solution)/shard_map/scan_and_blocks/pallas_call | solution.py:295
  29.3 1.8 %across_blocks.1 = (bf16[1280,256]{1,0:T(8,128)(2,1)}, bf16[1280,256]{1,0:T(8,128)(2,1)}, bf16[1280,256]{1,0:T(8,128)(2,1)}, bf16[1280,256]{1,0:T(8,128)(2,1)}) custom-call(bf16[1280,256]{1,0:T(8,128)(2,1)S(1)} %get-tuple-element.10.k, bf16[1280,256]{1,0:T(8,128)(2,1)S(1)} %get-tuple-element.11.v, bf16[2,1280,256]{2,1,0:T(8,128)(2,1)S(1)} %get-tuple-element.12.early, ...), custom_call_target="tpu_custom_call" | custom-call | tf_op jit(solution)/shard_map/across_blocks/pallas_call | solution.py:314

commit v5 on v4

--- a/solution.py
+++ b/solution.py
@@ -133,8 +133,8 @@
             return (group == half - 1) & (j >= half)
         return (group == half) & (near <= j < half)
 
-    def exchange(way):
-        for j in range(groups):
+    def exchange(way, those):
+        for j in those:
 
             @pl.when(direct(way, j))
             def _():
@@ -200,7 +200,7 @@
     states(k, v, BEFORE, range(blocks))
     scatter(BEFORE)
     collect(AFTER)
-    exchange(AFTER)
+    exchange(AFTER, range(half))
 
     @pl.when(group == half)
     def _():
@@ -208,6 +208,7 @@
         tell(higher_sem, at(half - 1, turned(half - 1, mine)))
 
     lax.fori_loop(0, 2, within, 0)
+    exchange(AFTER, range(half, groups))
     collect(BEFORE)
     higher = jnp.where(group < half - 1, half - 1 - group, jnp.where(group == half - 1, 1, groups - 1 - group))
 
@@ -215,7 +216,7 @@
     def _():
         pl.semaphore_wait(higher_sem, higher)
 
-    exchange(BEFORE)
+    exchange(BEFORE, range(groups))
 
     @pl.when(group < half)
     def _():

time: 31.3 us -> 31.4 us (level)
  the two profiles are of different devices: /device:TPU:68 before, /device:TPU:198 now
where the time goes in v5:
time: 31.4 us; the launch traced here: 31.2 us
  Pallas kernels  30.5 us (97%)
  between operations  0.64 us (2%)
    pallas_call x1, Pallas kernels, shards(): pl.pallas_call(functools.partial(carry_kernel, scale, groups), out_shape=...  28.8 us
    pallas_call x1, Pallas kernels, shards(): pl.pallas_call(functools.partial(final_kernel, scale), out_shape=(out,) *...  1.79 us

profile of v5, /device:TPU:198, one launch (start us, length us, event | category | flops | bytes accessed | tf_op | source)
XLA Modules:
  0.0 31.2 jit_solution(15614824573393706712)
XLA Ops:
  0.6 28.8 %scan_and_blocks.1 = (bf16[1280,256]{1,0:T(8,128)(2,1)S(1)}, bf16[1280,256]{1,0:T(8,128)(2,1)S(1)}, bf16[2,1280,256]{2,1,0:T(8,128)(2,1)S(1)}, f32[2,1280,256]{2...) custom-call(bf16[1280,256]{1,0:T(8,128)(2,1)} %q_hbm.1, bf16[1280,256]{1,0:T(8,128)(2,1)} %k_hbm.1, ...), custom_call_target="tpu_custom_call" | custom-call | tf_op jit(solution)/shard_map/scan_and_blocks/pallas_call | solution.py:296
  29.4 1.8 %across_blocks.1 = (bf16[1280,256]{1,0:T(8,128)(2,1)}, bf16[1280,256]{1,0:T(8,128)(2,1)}, bf16[1280,256]{1,0:T(8,128)(2,1)}, bf16[1280,256]{1,0:T(8,128)(2,1)}) custom-call(bf16[1280,256]{1,0:T(8,128)(2,1)S(1)} %get-tuple-element.10.k, bf16[1280,256]{1,0:T(8,128)(2,1)S(1)} %get-tuple-element.11.v, bf16[2,1280,256]{2,1,0:T(8,128)(2,1)S(1)} %get-tuple-element.12.early, ...), custom_call_target="tpu_custom_call" | custom-call | tf_op jit(solution)/shard_map/across_blocks/pallas_call | solution.py:315
